TPU v7x, 32 devices: a whole 2x2x4 slice. The times are simulated.
32 devices in a mesh: groups: 2 (over y), rows: 4 (over z), tensor: 2 (over x), sub: 2 (over core).
Axes of the slice: x: 2, y: 2, z: 4, core: 2. Of those that a mesh axis runs over, the one named last changes fastest.
Arguments:
- features: bfloat16 [512, 24576], P(('groups', 'rows'), ('tensor', 'sub')), parts along dimension 0, may hold values from -6 to 6
- fc_weight: bfloat16 [24576, 4096], P(('tensor', 'sub'), 'rows'), may hold values from -0.0390625 to 0.0390625
- counts: int32 [8], P('groups'), parts along dimension 0, may hold values from 1 to 128, 256 in all
- order: int32 [512], P('groups'), parts along dimension 0, may hold values from 0 to 255, each once
- norm_gain: float32 [4096], replicated, may hold values from 0.1 to 1.9
- target: bfloat16 [1024, 4096], P(('groups', 'rows', 'tensor', 'sub')), parts along dimension 0, may hold values from -6 to 6
Outputs:
- fc_grad: float32 [49152, 4096], P(('groups', 'tensor', 'sub'), 'rows'), parts along dimension 0
- loss_slots: float32 [1024], P(('groups', 'rows', 'tensor', 'sub')), parts along dimension 0
There are 2 independent parts, one for each index of `groups`. A program takes and returns all parts, laid end to end along the dimension named above; an argument that names none is the same for every part. Nothing has to cross between parts.
Inputs may be any that keep to these rules, and one draw needn't show every extreme that they name: counts sum to 256; the largest is exactly 128. `order`: each position appears exactly once.
All inputs are finite; a program needn't handle non-finite values.
Results may differ from a plain program's by a relative error of at most 0.0029.
Values may be sent and summed in bfloat16 or wider, within the bound.
A program may use at most 192 MiB of HBM per device.

v0:
```python
import math

import jax
import jax.numpy as jnp
from jax import lax
from jax.sharding import PartitionSpec as P


def on_device(features, fc_weight, counts, order, norm_gain, target):
    group = lax.axis_size(("tensor", "sub"))
    share = target.shape[0]
    cap = share * group
    total = order.shape[0]
    columns = fc_weight.shape[1]
    offsets = jnp.cumsum(counts) - counts
    index = jnp.arange(cap, dtype=jnp.int32)
    live = index[None, :] < counts[:, None]
    spot = jnp.minimum(offsets[:, None] + index[None, :], total - 1)
    slot_pos = jnp.take(order, spot)
    member = lax.axis_index(("tensor", "sub"))
    my_live = lax.dynamic_slice_in_dim(live, member * share, share, 1)
    live_here = lax.dynamic_index_in_dim(my_live, lax.axis_index("rows"), 0, keepdims=False)
    all_features = lax.all_gather(features, "rows", axis=0, tiled=True)
    joined = jnp.dot(all_features, fc_weight, preferred_element_type=jnp.float32)
    picked = jnp.where(live[:, :, None], jnp.take(joined, slot_pos, axis=0), jnp.float32(0))
    arrived = lax.all_to_all(picked, "rows", split_axis=0, concat_axis=2, tiled=True)
    hidden = lax.psum_scatter(arrived, ("tensor", "sub"), scatter_dimension=1, tiled=True)[0]
    rstat = lax.rsqrt(jnp.mean(hidden * hidden, axis=1, keepdims=True) + 1e-06)
    normed = hidden * rstat * norm_gain
    err = normed - target.astype(jnp.float32)
    loss_slots = jnp.where(live_here, jnp.mean(err * err, axis=1), jnp.float32(0))
    dnormed = jnp.where(live_here[:, None], err, jnp.float32(0)) / math.sqrt(total)
    scaled = norm_gain * dnormed
    dhidden = rstat * scaled - hidden * rstat * rstat * rstat * jnp.mean(
        scaled * hidden, axis=1, keepdims=True
    )
    dhidden = dhidden.astype(jnp.bfloat16)
    returned = lax.all_to_all(dhidden[None], "rows", split_axis=2, concat_axis=0, tiled=True)
    every = lax.all_gather(returned, ("tensor", "sub"), axis=1, tiled=True)
    target_rows = jnp.where(live, slot_pos, total)
    grad_rows = jnp.zeros((total, columns), jnp.bfloat16).at[target_rows].set(every, mode="drop")
    fc_grad = lax.dot_general(
        all_features, grad_rows, (((0,), (0,)), ((), ())), preferred_element_type=jnp.float32
    )
    return (fc_grad, loss_slots)


def solution(mesh):
    return jax.shard_map(
        on_device,
        mesh=mesh,
        in_specs=(
            P(("groups", "rows"), ("tensor", "sub")),
            P(("tensor", "sub"), "rows"),
            P("groups"),
            P("groups"),
            P(),
            P(("groups", "rows", "tensor", "sub"), None),
        ),
        out_specs=(P(("groups", "tensor", "sub"), "rows"), P(("groups", "rows", "tensor", "sub"))),
        check_vma=False,
    )
```

profile of v0, /device:TPU:0, one launch (start us, length us, event | category | flops | bytes accessed | tf_op | source)
XLA Modules:
  0.0 280.5 jit_solution(5500177641752919583)
XLA Ops:
  7.2 0.0 copy-start
  7.2 0.0 all-gather.4.cloned.1.call-start
  7.2 0.7 all-gather.4.cloned.1.call-update
  7.9 0.0 reduce-scatter.2.cloned.1.call-start
  8.0 0.8 reduce-window.9
  8.8 0.7 bitcast_subtract_fusion
  9.4 0.1 fusion.7
  9.5 0.0 copy-done
  9.5 3.5 %gather_fusion = s32[512]{0:T(512)S(1)} fusion(s32[256]{0:T(256)S(1)} %copy-done, s32[1024]{0:T(1024)S(1)} %pad_clamp_fusion.1), kind=kCustom, calls=%fused_computation | custom fusion | bytes 6144 | tf_op jit(solution)/shard_map/jit(_take)/gather | solution.py:19
  13.1 0.7 fusion.6
  13.8 0.7 iota_compare_fusion
  14.5 61.3 %all-gather.4.cloned.1.call-done = bf16[256,6144]{1,0:T(8,128)(2,1)} async-done(((bf16[64,6144]{1,0:T(8,128)(2,1)}), bf16[256,6144]{1,0:T(8,128)(2,1)}) %all-gather.4.cloned.1.call-update) | async-done | bytes 3145744 | tf_op jit(solution)/shard_map/all_gather | solution.py:23
  75.8 7.3 %fusion.8 = f32[256,1024]{1,0:T(8,128)S(1)} fusion(bf16[256,6144]{1,0:T(8,128)(2,1)} %all-gather.4.cloned.1.call-done, bf16[6144,1024]{1,0:T(8,128)(2,1)} %param.7), kind=kOutput, calls=%fused_computation.38 | convolution fusion | flops 3221225472 | bytes 16777216 | tf_op jit(solution)/shard_map/dot_general | solution.py:24
  83.1 1.9 gather_fusion.1
  85.1 0.3 select_select_fusion
  85.4 50.9 %all_to_all.36 = f32[4,128,1024]{2,1,0:T(8,128)S(1)} all-to-all(f32[4,128,1024]{2,1,0:T(8,128)S(1)} %select_select_fusion), channel_id=1, replica_groups=mesh['groups'=2,'rows'=4,'tensor'=2,'sub'=2] {'rows'}, dimensions={0} | all-to-all | bytes 4194304 | tf_op jit(solution)/shard_map/all_to_all | solution.py:26
  136.3 0.0 copy-start.4
  136.3 0.0 copy-start.3
  136.3 1.5 copy.27
  137.7 0.0 reduce-scatter.2.cloned.1.call-update
  137.7 0.0 all-gather.6.cloned.1.call-start
  137.8 0.1 dynamic-slice_bitcast_fusion
  137.9 0.0 copy-done.4
  137.9 30.5 %reduce-scatter.2.cloned.1.call-done = f32[1,32,4096]{2,1,0:T(8,128)} async-done(((f32[1,128,4096]{2,1,0:T(8,128)}), f32[1,32,4096]{2,1,0:T(8,128)}) %reduce-scatter.2.cloned.1.call-update) | async-done | bytes 524304 | tf_op jit(solution)/shard_map/reduce_scatter | solution.py:27
  168.4 1.2 fusion
  169.6 0.0 copy-done.3
  169.6 1.4 multiply_reduce_fusion
  171.0 1.3 fusion.4
  172.3 2.8 copy.22
  175.1 0.5 broadcast.294
  175.6 22.4 %reduce = bf16[4096,32]{1,0:T(8,128)(2,1)S(1)} reduce(bf16[4096,1,32]{2,1,0:T(2,128)(2,1)S(1)} %bitcast.69, bf16[]{:T(256)} %broadcast.294), dimensions={1}, to_apply=%bitcast.57.reduce_sub_computation | reduce | bytes 524290
  198.0 1.0 reshape.275
  199.0 13.3 %all_to_all.37 = bf16[4,2,16384]{2,1,0:T(2,128)(2,1)S(1)} all-to-all(bf16[4,2,16384]{2,1,0:T(2,128)(2,1)S(1)} %reshape.275), channel_id=1, replica_groups=mesh['groups'=2,'rows'=4,'tensor'=2,'sub'=2] {'rows'}, dimensions={0} | all-to-all | bytes 524288 | tf_op jit(solution)/shard_map/all_to_all | solution.py:38
  212.2 1.0 reshape.276
  213.3 2.1 copy.23
  215.4 0.0 copy-start.2
  215.4 0.9 all_to_all.31
  216.3 0.0 all-gather.6.cloned.1.call-update
  216.3 0.6 multiply_select_fusion
  216.9 14.4 %all-gather.6.cloned.1.call-done = bf16[4,1,128,1024]{3,0,1,2:T(4,128)(2,1)} async-done(((bf16[4,1,32,1024]{3,0,1,2:T(4,128)(2,1)}), bf16[4,1,128,1024]{3,0,1,2:T(4,128)(2,1)}) %all-gather.6.cloned.1.call-update) | async-done | bytes 1048592 | tf_op jit(solution)/shard_map/all_gather | solution.py:39
  231.3 2.5 copy.25
  233.8 4.2 %scatter_custom_fusion = bf16[256,1024]{1,0:T(8,128)(2,1)} fusion(s32[512]{0:T(512)S(1)} %get-tuple-element.15, bf16[512,1024]{1,0:T(8,128)(2,1)} %bitcast.71, bf16[]{:T(256)} %constant.67.clone.1), kind=kCustom, calls=%fused_computation.14 | custom fusion | bytes 524800 | tf_op jit(solution)/shard_map/scatter | solution.py:41
  238.0 0.0 copy-done.2
  238.0 11.2 %convolution_bitcast_fusion = f32[6144,1024]{0,1:T(8,128)} fusion(bf16[256,1024]{1,0:T(8,128)(2,1)} %scatter_custom_fusion, bf16[256,6144]{1,0:T(8,128)(2,1)S(1)} %copy-done.2), kind=kOutput, calls=%fused_computation.3 | convolution fusion | flops 3221225472 | bytes 28835840 | tf_op jit(solution)/shard_map/dot_general | solution.py:42
  249.2 0.0 copy-start.1
  249.2 24.7 %copy.26 = f32[6144,1024]{1,0:T(8,128)} copy(f32[6144,1024]{0,1:T(8,128)} %convolution_bitcast_fusion) | data formatting | bytes 50331648
  273.9 0.0 copy-done.1
  (5 shorter events, 0.0 us)
Async XLA Ops:
  7.2 2.4 copy-start
  7.2 68.6 %all-gather.4.cloned.1.call-start = ((), (), s32[]{:S(2)}) async-start(), calls=%async_computation.3 | async-start | bytes 3932160 | tf_op jit(solution)/shard_map/all_gather | solution.py:23
  7.9 160.5 %reduce-scatter.2.cloned.1.call-start = ((), (), s32[]{:S(2)}) async-start(), calls=%async_computation.4 | async-start | bytes 2621440 | tf_op jit(solution)/shard_map/reduce_scatter | solution.py:27
  136.3 1.6 copy-start.4
  136.3 33.3 %copy-start.3 = (bf16[32,4096]{1,0:T(8,128)(2,1)S(1)}, bf16[32,4096]{1,0:T(8,128)(2,1)}, u32[]{:S(2)}) copy-start(bf16[32,4096]{1,0:T(8,128)(2,1)} %param.11) | copy-start | bytes 786436
  137.7 93.6 %all-gather.6.cloned.1.call-start = ((), (), s32[]{:S(2)}) async-start(), calls=%async_computation.5 | async-start | bytes 1310720 | tf_op jit(solution)/shard_map/all_gather | solution.py:39
  215.4 22.6 %copy-start.2 = (bf16[256,6144]{1,0:T(8,128)(2,1)S(1)}, bf16[256,6144]{1,0:T(8,128)(2,1)}, u32[]{:S(2)}) copy-start(bf16[256,6144]{1,0:T(8,128)(2,1)} %all-gather.4.cloned.1.call-done) | copy-start | bytes 9437188
  249.2 24.7 %copy-start.1 = (s32[256]{0:T(256)S(1)}, s32[256]{0:T(256)}, u32[]{:S(2)}) copy-start(s32[256]{0:T(256)} %param.9) | copy-start | bytes 3076
Sparse Core Ops, SparseCore 0:
  9.6 66.1 all-gather.3
  137.9 30.4 reduce-scatter.1
  216.4 14.8 all-gather.5
where the time goes:
time: 281 us; the launch traced here: 280 us
  waiting for transfers between devices  107 us (38%)
  blocking collectives  64.2 us (23%)
  local copies, waits for them, and re-layouts  46.6 us (17%)
  other arithmetic  30.2 us (11%)
  matrix products  18.6 us (7%)
  between operations  13.9 us (5%)
    all_gather x1, waiting for transfers between devices, on_device(): all_features = lax.all_gather(features, 'rows', axis=0, tiled=True)  61.3 us
    all_to_all x1, blocking collectives, on_device(): lax.all_to_all(picked, 'rows', split_axis=0, concat_axis=2, tiled=True)  50.9 us
    reduce_scatter x1, waiting for transfers between devices, on_device(): lax.psum_scatter(arrived, ('tensor', 'sub'), scatter_dimension=1, tiled=T...  30.5 us
    unnamed x14, local copies, waits for them, and re-layouts  27.3 us
    unnamed x1, other arithmetic  22.4 us
    all_gather x1, waiting for transfers between devices, on_device(): every = lax.all_gather(returned, ('tensor', 'sub'), axis=1, tiled=True)  14.4 us
    all_to_all x1, blocking collectives, on_device(): lax.all_to_all(dhidden[None], 'rows', split_axis=2, concat_axis=0, tiled=...  13.3 us
    dot_general x1, matrix products, on_device(): lax.dot_general(all_features, grad_rows, (((0,), (0,)), ((), ())), prefer...  11.2 us
  transfers between devices with their start and end apart: 3, of which 3 were waited for; matrix products, arithmetic and copies ran while one was open for 3% of the time, Pallas kernels for 0%

commit v1 on v0

v1 whole, which is shorter than its diff:
```python
import functools
import math

import jax
import jax.numpy as jnp
from jax import lax
from jax.experimental import pallas as pl
from jax.experimental.pallas import tpu as pltpu
from jax.sharding import PartitionSpec as P

MESH = pl.DeviceIdType.MESH
F32 = jnp.float32
BF16 = jnp.bfloat16
CHUNKS = 4


def kernel(
    R, T, S, direct,
    counts_ref, order_ref, gain_ref, feat_in, w_in, target_in,
    feat_out, grad_out, loss_out,
    feat, w, acc, rs, tall, hid, tsel, stats, ag, lp, lz, lm,
    w_sem, own_sem, out_sem, f_send, f_recv, rs_send, rs_recv,
    tz_send, tz_recv, tm_send, tm_recv, st_send, st_recv,
    ag_send, ag_recv, lz_send, lz_recv, lm_send, lm_recv, tl_sem,
):
    M = T * S
    rows = feat.shape[2]
    part = feat.shape[3]
    cols = w.shape[2]
    pm = rows // M
    mine = R * pm
    share = target_in.shape[0]
    cap = share * M
    total = order_ref.shape[1]
    z = lax.axis_index("rows")
    t = lax.axis_index("tensor")
    s_ = lax.axis_index("sub")
    m = t * S + s_

    def member(j):
        q = lax.rem(m + j, M)
        return q, {"tensor": q // S, "sub": lax.rem(q, S)}

    def zpeer(j):
        q = lax.rem(z + j, R)
        return q, {"rows": q}

    def each_z(body):
        if R <= 4:
            for j in range(1, R):
                body(j)
        else:
            @pl.loop(1, R)
            def _(j):
                body(j)

    def w_copy(q):
        return pltpu.make_async_copy(w_in.at[pl.ds(q * part, part)], w.at[q], w_sem.at[q])

    def own_copy(q):
        return pltpu.make_async_copy(
            feat_in.at[:, pl.ds(q * part, part)], feat.at[z, q], own_sem.at[q])

    for q in range(CHUNKS):
        own_copy(q).start()
    own_cols = pl.ds(pl.multiple_of(z * cols, 128), cols)
    own_t = pltpu.make_async_copy(target_in.at[:, own_cols], tall.at[m, z], tl_sem.at[0])
    own_t.start()
    for q in range(CHUNKS):
        w_copy(q).start()

    barrier = pltpu.get_barrier_semaphore()

    def hello(j):
        _, dev = zpeer(j)
        pl.semaphore_signal(barrier, inc=1, device_id=dev, device_id_type=MESH)

    each_z(hello)
    for j in range(1, M):
        _, dev = member(j)
        pl.semaphore_signal(barrier, inc=1, device_id=dev, device_id_type=MESH)
    pl.semaphore_wait(barrier, R - 1 + M - 1)

    def f_copy(way, s, q):
        to = jnp.clip(z - 1 if way == 0 else z + 1, 0, R - 1)
        return pltpu.make_async_remote_copy(
            src_ref=feat.at[s, q], dst_ref=feat.at[s, q],
            send_sem=f_send.at[way, s, q], recv_sem=f_recv.at[s, q],
            device_id={"rows": to}, device_id_type=MESH)

    def out_copy(s, q):
        return pltpu.make_async_copy(
            feat.at[s, q],
            feat_out.at[pl.ds(pl.multiple_of(s * rows, rows), rows), pl.ds(q * part, part)],
            out_sem.at[s, q])

    def tz_copy(src, dst, dev):
        columns = pl.ds(pl.multiple_of(dst * cols, 128), cols)
        return pltpu.make_async_remote_copy(
            src_ref=target_in.at[:, columns], dst_ref=tall.at[m, src],
            send_sem=tz_send.at[dst], recv_sem=tz_recv.at[src],
            device_id=dev, device_id_type=MESH)

    def tm_copy(src, dst, dev):
        return pltpu.make_async_remote_copy(
            src_ref=tall.at[src], dst_ref=tall.at[src],
            send_sem=tm_send.at[dst], recv_sem=tm_recv.at[src],
            device_id=dev, device_id_type=MESH)

    def rs_copy(s, src, dst, dev):
        return pltpu.make_async_remote_copy(
            src_ref=acc.at[s, pl.ds(pl.multiple_of(dst * pm, pm), pm)], dst_ref=rs.at[s, src],
            send_sem=rs_send.at[s, dst], recv_sem=rs_recv.at[s, src],
            device_id=dev, device_id_type=MESH)

    def st_copy(src, dst, dev):
        return pltpu.make_async_remote_copy(
            src_ref=stats.at[src], dst_ref=stats.at[src],
            send_sem=st_send.at[dst], recv_sem=st_recv.at[src],
            device_id=dev, device_id_type=MESH)

    def ag_copy(src, dst, dev):
        return pltpu.make_async_remote_copy(
            src_ref=ag.at[src], dst_ref=ag.at[src],
            send_sem=ag_send.at[dst], recv_sem=ag_recv.at[src],
            device_id=dev, device_id_type=MESH)

    def lz_copy(src, dst, dev):
        return pltpu.make_async_remote_copy(
            src_ref=lp.at[dst], dst_ref=lz.at[src],
            send_sem=lz_send.at[dst], recv_sem=lz_recv.at[src],
            device_id=dev, device_id_type=MESH)

    def lm_copy(src, dst, dev):
        return pltpu.make_async_remote_copy(
            src_ref=lm.at[src], dst_ref=lm.at[src],
            send_sem=lm_send.at[dst], recv_sem=lm_recv.at[src],
            device_id=dev, device_id_type=MESH)

    for q in range(CHUNKS):
        own_copy(q).wait()

        @pl.when(z > 0)
        def _():
            f_copy(0, z, q).start()

        @pl.when(z < R - 1)
        def _():
            f_copy(1, z, q).start()

        out_copy(z, q).start()

    def send_target(j):
        dst, dev = zpeer(j)
        tz_copy(z, dst, dev).start()

    each_z(send_target)

    def multiply(s, q):
        piece = jnp.dot(feat[s, q], w[q], preferred_element_type=F32)
        if q == 0:
            acc[s] = piece
        else:
            acc[s] += piece

    def send_sums(s):
        for j in range(1, M):
            dst, dev = member(j)
            rs_copy(s, m, dst, dev).start()

    for q in range(CHUNKS):
        w_copy(q).wait()
        multiply(z, q)
    send_sums(z)

    def step(d):
        left, right = z - d, z + d
        for q in range(CHUNKS):
            @pl.when(right < R)
            def _():
                f_copy(0, right, q).wait_recv()

                @pl.when(z > 0)
                def _():
                    f_copy(0, right, q).start()

                out_copy(right, q).start()

            @pl.when(left >= 0)
            def _():
                f_copy(1, left, q).wait_recv()

                @pl.when(z < R - 1)
                def _():
                    f_copy(1, left, q).start()

                out_copy(left, q).start()
                multiply(left, q)

            @pl.when(right < R)
            def _():
                multiply(right, q)

        @pl.when(left >= 0)
        def _():
            send_sums(left)

        @pl.when(right < R)
        def _():
            send_sums(right)

    def target_out():
        own_t.wait()

        def arrived(j):
            src, dev = zpeer(j)
            tz_copy(src, z, dev).wait_recv()

        each_z(arrived)
        for j in range(1, M):
            dst, dev = member(j)
            tm_copy(m, dst, dev).start()

    step(1)
    target_out()

    row = lax.broadcasted_iota(jnp.int32, (mine, total), 0)
    position = (row // pm) * rows + m * pm + lax.rem(row, pm)
    rank = lax.broadcasted_iota(jnp.int32, (1, total), 1)
    trainer = jnp.zeros((1, total), jnp.int32)
    start = jnp.zeros((1, total), jnp.int32)
    end = jnp.int32(0)
    for r in range(R):
        n = counts_ref[r]
        end = end + n
        past = rank >= end
        trainer = trainer + jnp.where(past, 1, 0)
        start = start + jnp.where(past, n, 0)
    natural = trainer * cap + rank - start
    slot = jnp.sum(jnp.where(order_ref[...] == position, natural, 0), axis=1, keepdims=True)

    def step_loop(d, c):
        step(d)
        return c

    if R > 3:
        lax.fori_loop(2, R - 1, step_loop, 0)

    for j in range(1, M):
        src, dev = member(j)
        tm_copy(src, m, dev).wait_recv()
    trn = slot // cap
    inside = slot - trn * cap
    owner = inside // share
    place = owner * (R * share) + trn * share + (inside - owner * share)
    seat = lax.broadcasted_iota(jnp.int32, (mine, M * R * share), 1)
    pick = jnp.where(seat == place, F32(1), F32(0)).astype(BF16)
    tsel[...] = jnp.dot(
        pick, tall[...].reshape(M * R * share, cols), preferred_element_type=F32)

    if R > 2:
        step(R - 1)

    gain = gain_ref[:, own_cols]
    lane = lax.broadcasted_iota(jnp.int32, (pm, 128), 1)

    def collect(s, c):
        h = acc[s, pl.ds(pl.multiple_of(m * pm, pm), pm)]
        for j in range(1, M):
            src, dev = member(j)
            rs_copy(s, src, m, dev).wait_recv()
            h = h + rs[s, src]
        here = pl.ds(pl.multiple_of(s * pm, pm), pm)
        hid[here] = h
        gh = gain * h
        a = jnp.sum(h * h, axis=1, keepdims=True)
        b = jnp.sum(gh * gh, axis=1, keepdims=True)
        e = jnp.sum(gh * tsel[here], axis=1, keepdims=True)
        stats[z, here] = jnp.where(lane == 0, a, jnp.where(lane == 1, b, e))
        return c

    lax.fori_loop(0, R, collect, 0)

    def send_stats(j):
        dst, dev = zpeer(j)
        st_copy(z, dst, dev).start()

    each_z(send_stats)

    def got_stats(j):
        src, dev = zpeer(j)
        st_copy(src, z, dev).wait_recv()

    each_z(got_stats)
    summed = jnp.sum(stats[...], axis=0)
    depth = R * cols
    a, b, e = summed[:, 0:1], summed[:, 1:2], summed[:, 2:3]
    rstat = lax.rsqrt(a / depth + 1e-06)
    scale = 1.0 / math.sqrt(total)
    dotted = (rstat * b - e) * (scale / depth)
    h = hid[...]
    err = h * rstat * gain - tsel[...]
    dh = rstat * (gain * (err * scale)) - h * (rstat * rstat * rstat * dotted)
    ag[m] = dh.astype(BF16)
    for j in range(1, M):
        dst, dev = member(j)
        ag_copy(m, dst, dev).start()

    loss = jnp.sum(err * err, axis=1, keepdims=True) / depth
    seat1 = lax.broadcasted_iota(jnp.int32, (mine, cap), 1)

    def scatter(r, c):
        one = jnp.sum(
            jnp.where(slot - r * cap == seat1, loss, F32(0)), axis=0, keepdims=True)
        lp[r] = jnp.broadcast_to(one, (8, cap))
        return c

    lax.fori_loop(0, R, scatter, 0)

    def send_loss(j):
        dst, dev = zpeer(j)
        lz_copy(z, dst, dev).start()

    each_z(send_loss)
    lz[z] = lp[z]

    def got_loss(j):
        src, dev = zpeer(j)
        lz_copy(src, z, dev).wait_recv()

    each_z(got_loss)
    lm[m] = jnp.sum(lz[...], axis=0)
    for j in range(1, M):
        dst, dev = member(j)
        lm_copy(m, dst, dev).start()

    for j in range(1, M):
        src, dev = member(j)
        ag_copy(src, m, dev).wait_recv()
    if direct:
        for q in range(M):
            for s in range(R):
                grad_out[s * rows + q * pm:s * rows + (q + 1) * pm] = ag[q, s * pm:(s + 1) * pm]
    else:
        grad_out[...] = ag[...]
    for j in range(1, M):
        src, dev = member(j)
        lm_copy(src, m, dev).wait_recv()
    loss_out[...] = jnp.sum(lm[...], axis=0)

    def sent(s, c):
        for q in range(CHUNKS):
            out_copy(s, q).wait()

            @pl.when(jnp.logical_and(s >= z, z > 0))
            def _():
                f_copy(0, s, q).wait_send()

            @pl.when(jnp.logical_and(s <= z, z < R - 1))
            def _():
                f_copy(1, s, q).wait_send()

        for j in range(1, M):
            dst, dev = member(j)
            rs_copy(s, m, dst, dev).wait_send()
        return c

    lax.fori_loop(0, R, sent, 0)
    for j in range(1, M):
        dst, dev = member(j)
        tm_copy(m, dst, dev).wait_send()
        ag_copy(m, dst, dev).wait_send()
        lm_copy(m, dst, dev).wait_send()

    def sent_z(j):
        dst, dev = zpeer(j)
        tz_copy(z, dst, dev).wait_send()
        st_copy(z, dst, dev).wait_send()
        lz_copy(z, dst, dev).wait_send()

    each_z(sent_z)


def on_device(features, fc_weight, counts, order, norm_gain, target):
    R = lax.axis_size("rows")
    T = lax.axis_size("tensor")
    S = lax.axis_size("sub")
    M = T * S
    rows, depth = features.shape
    cols = fc_weight.shape[1]
    total = order.shape[0]
    share = target.shape[0]
    cap = share * M
    part = depth // CHUNKS
    pm = rows // M
    mine = R * pm
    direct = pm % 16 == 0
    any_ = pl.BlockSpec(memory_space=pl.ANY)
    vmem = pl.BlockSpec(memory_space=pltpu.VMEM)
    smem = pl.BlockSpec(memory_space=pltpu.SMEM)
    dma = pltpu.SemaphoreType.DMA
    grad_shape = (total, cols) if direct else (M, mine, cols)
    all_features, grad, loss = pl.pallas_call(
        functools.partial(kernel, R, T, S, direct),
        out_shape=(
            jax.ShapeDtypeStruct((total, depth), BF16),
            jax.ShapeDtypeStruct(grad_shape, BF16),
            jax.ShapeDtypeStruct((8, cap), F32),
        ),
        in_specs=[smem, vmem, vmem, any_, any_, any_],
        out_specs=(any_, vmem, vmem),
        scratch_shapes=[
            pltpu.VMEM((R, CHUNKS, rows, part), BF16),
            pltpu.VMEM((CHUNKS, part, cols), BF16),
            pltpu.VMEM((R, rows, cols), F32),
            pltpu.VMEM((R, M, pm, cols), F32),
            pltpu.VMEM((M, R, share, cols), BF16),
            pltpu.VMEM((mine, cols), F32),
            pltpu.VMEM((mine, cols), F32),
            pltpu.VMEM((R, mine, 128), F32),
            pltpu.VMEM((M, mine, cols), BF16),
            pltpu.VMEM((R, 8, cap), F32),
            pltpu.VMEM((R, 8, cap), F32),
            pltpu.VMEM((M, 8, cap), F32),
            dma((CHUNKS,)), dma((CHUNKS,)), dma((R, CHUNKS)),
            dma((2, R, CHUNKS)), dma((R, CHUNKS)),
            dma((R, M)), dma((R, M)),
            dma((R,)), dma((R,)), dma((M,)), dma((M,)),
            dma((R,)), dma((R,)), dma((M,)), dma((M,)),
            dma((R,)), dma((R,)), dma((M,)), dma((M,)), dma((1,)),
        ],
        compiler_params=pltpu.CompilerParams(
            collective_id=0, has_side_effects=True, vmem_limit_bytes=48 * 1024 * 1024),
        name="gather_join_norm",
    )(counts, order[None, :], norm_gain[None, :], features, fc_weight, target)
    if not direct:
        grad = grad.reshape(M, R, pm, cols).transpose(1, 0, 2, 3).reshape(total, cols)
    member = lax.axis_index("tensor") * S + lax.axis_index("sub")
    loss_slots = lax.dynamic_slice_in_dim(loss[0], member * share, share, 0)
    fc_grad = lax.dot_general(
        all_features, grad, (((0,), (0,)), ((), ())), preferred_element_type=F32)
    return (fc_grad, loss_slots)


def solution(mesh):
    return jax.shard_map(
        on_device,
        mesh=mesh,
        in_specs=(
            P(("groups", "rows"), ("tensor", "sub")),
            P(("tensor", "sub"), "rows"),
            P("groups"),
            P("groups"),
            P(),
            P(("groups", "rows", "tensor", "sub"), None),
        ),
        out_specs=(P(("groups", "tensor", "sub"), "rows"), P(("groups", "rows", "tensor", "sub"))),
        check_vma=False,
    )
```

time: 281 us -> 97 us (0.35)
  waiting for transfers between devices: 107 us -> 0 us
  Pallas kernels: 0 us -> 80.5 us
  blocking collectives: 64.2 us -> 0 us
  local copies, waits for them, and re-layouts: 46.6 us -> 4.72 us
  other arithmetic: 30.2 us -> 0 us
  between operations: 13.9 us -> 0.67 us
  matrix products: 18.6 us -> 10.8 us
    pallas_call x0 -> x1, Pallas kernels: none -> 80.5 us  [on_device(): pl.pallas_call(functools.partial(kernel, R, T, S, direct), out_shape=(jax...]
    all_gather x2 -> x0, waiting for transfers between devices: 75.7 us -> none  [the longest x1 61.3 us: on_device(): all_features = lax.all_gather(features, 'rows', axis=0, tiled=True)]
    all_to_all x2 -> x0, blocking collectives: 64.2 us -> none  [the longest x1 50.9 us: on_device(): lax.all_to_all(picked, 'rows', split_axis=0, concat_axis=2, tiled=True)]
    reduce_scatter x1 -> x0, waiting for transfers between devices: 30.5 us -> none  [on_device(): lax.psum_scatter(arrived, ('tensor', 'sub'), scatter_dimension=1, tiled=T...]
    unnamed x14 -> x10, local copies, waits for them, and re-layouts: 27.3 us -> 4.13 us
    unnamed x1 -> x0, other arithmetic: 22.4 us -> none
    dot_general x2 -> x1, matrix products: 18.6 us -> 10.8 us  [on_device(): lax.dot_general(all_features, grad, (((0,), (0,)), ((), ())), preferred_e...]
    gather x2 -> x0, local copies, waits for them, and re-layouts: 5.44 us -> none  [the longest x1 3.52 us: on_device(): slot_pos = jnp.take(order, spot)]
  transfers between devices with their start and end apart: 3 -> 0, of which waited for: 3 -> 0; matrix products, arithmetic and copies ran while one was open for 3% -> 0% of each run, Pallas kernels for 0% -> 0%
where the time goes in v1:
time: 97 us; the launch traced here: 96.7 us
  Pallas kernels  80.5 us (83%)
  matrix products  10.8 us (11%)
  local copies, waits for them, and re-layouts  4.72 us (5%)
    pallas_call x1, Pallas kernels, on_device(): pl.pallas_call(functools.partial(kernel, R, T, S, direct), out_shape=(jax...  80.5 us
    dot_general x1, matrix products, on_device(): lax.dot_general(all_features, grad, (((0,), (0,)), ((), ())), preferred_e...  10.8 us
    unnamed x10, local copies, waits for them, and re-layouts  4.13 us

profile of v1, /device:TPU:0, one launch (start us, length us, event | category | flops | bytes accessed | tf_op | source)
XLA Modules:
  0.0 96.7 jit_solution(18048211433483736274)
XLA Ops:
  0.6 0.0 copy-start
  0.6 1.1 %copy-done = bf16[64,6144]{1,0:T(8,128)(2,1)S(1)} copy-done((bf16[64,6144]{1,0:T(8,128)(2,1)S(1)}, bf16[64,6144]{1,0:T(8,128)(2,1)}, u32[]{:S(2)}) %copy-start) | copy-done | bytes 786456
  1.8 0.0 copy-start.1
  1.8 0.9 copy-done.1
  2.7 0.0 copy-start.2
  2.7 0.7 copy-done.2
  3.4 0.0 copy-start.3
  3.4 0.7 copy-done.3
  4.1 0.0 copy-start.4
  4.1 0.7 copy-done.4
  4.8 80.5 %gather_join_norm.1 = (bf16[256,6144]{1,0:T(8,128)(2,1)S(1)}, bf16[256,1024]{1,0:T(8,128)(2,1)S(1)}, f32[8,128]{1,0:T(8,128)S(1)}) custom-call(s32[4]{0:T(128)S(1)} %copy-done.4, s32[1,256]{1,0:T(1,128)S(1)} %bitcast.7, f32[1,4096]{1,0:T(1,128)S(1)} %bitcast.6, bf16[64,6144]{1,0:T(8,128)(2,1)S(1)} %copy-done, bf16[6144,1024]{1,0:T(8,128)(2,1)} %w_in.1, ...), custom_call_target="tpu_custom_call" | custom-call | tf_op jit(solution)/shard_map/gather_join_norm/pallas_call | solution.py:403
  85.3 0.6 dynamic-slice_bitcast_fusion
  85.9 10.8 %fusion = f32[6144,1024]{1,0:T(8,128)} fusion(bf16[256,6144]{1,0:T(8,128)(2,1)S(1)} %get-tuple-element.5, bf16[256,1024]{1,0:T(8,128)(2,1)S(1)} %get-tuple-element.6), kind=kOutput, calls=%fused_computation.1 | convolution fusion | flops 3221225472 | bytes 28835840 | tf_op jit(solution)/shard_map/dot_general | solution.py:440
  (1 shorter events, 0.0 us)
Async XLA Ops:
  0.6 1.1 %copy-start = (bf16[64,6144]{1,0:T(8,128)(2,1)S(1)}, bf16[64,6144]{1,0:T(8,128)(2,1)}, u32[]{:S(2)}) copy-start(bf16[64,6144]{1,0:T(8,128)(2,1)} %feat_in.1) | copy-start | bytes 2359300
  1.8 0.9 copy-start.1
  2.7 0.7 copy-start.2
  3.4 0.7 copy-start.3
  4.1 0.7 copy-start.4

commit v2 on v1

--- a/solution.py
+++ b/solution.py
@@ -15,11 +15,12 @@
 
 
 def kernel(
-    R, T, S, direct,
-    counts_ref, order_ref, gain_ref, feat_in, w_in, target_in,
+    R, T, S,
+    counts_in, order_in, gain_in, feat_in, w_in, target_in,
     feat_out, grad_out, loss_out,
-    feat, w, acc, rs, tall, hid, tsel, stats, ag, lp, lz, lm,
-    w_sem, own_sem, out_sem, f_send, f_recv, rs_send, rs_recv,
+    counts_ref, order_ref, gain_ref,
+    feat, w, acc, rs, xs, tall, hid, tsel, rowsum, stats, ag, lp, lz, lm,
+    w_sem, own_sem, out_sem, f_send, f_recv, rs_send, rs_recv, xs_send, xs_recv,
     tz_send, tz_recv, tm_send, tm_recv, st_send, st_recv,
     ag_send, ag_recv, lz_send, lz_recv, lm_send, lm_recv, tl_sem,
 ):
@@ -27,11 +28,11 @@
     rows = feat.shape[2]
     part = feat.shape[3]
     cols = w.shape[2]
-    pm = rows // M
+    pm = rows // S
     mine = R * pm
     share = target_in.shape[0]
     cap = share * M
-    total = order_ref.shape[1]
+    total = order_in.shape[1]
     z = lax.axis_index("rows")
     t = lax.axis_index("tensor")
     s_ = lax.axis_index("sub")
@@ -40,6 +41,14 @@
     def member(j):
         q = lax.rem(m + j, M)
         return q, {"tensor": q // S, "sub": lax.rem(q, S)}
+
+    def core(j):
+        q = lax.rem(s_ + j, S)
+        return q, {"sub": q}
+
+    def across(j):
+        q = lax.rem(t + j, T)
+        return q, {"tensor": q}
 
     def zpeer(j):
         q = lax.rem(z + j, R)
@@ -66,6 +75,13 @@
     own_cols = pl.ds(pl.multiple_of(z * cols, 128), cols)
     own_t = pltpu.make_async_copy(target_in.at[:, own_cols], tall.at[m, z], tl_sem.at[0])
     own_t.start()
+    small = (
+        pltpu.make_async_copy(counts_in, counts_ref, tl_sem.at[1]),
+        pltpu.make_async_copy(order_in, order_ref, tl_sem.at[2]),
+        pltpu.make_async_copy(gain_in.at[:, own_cols], gain_ref, tl_sem.at[3]),
+    )
+    for c in small:
+        c.start()
     for q in range(CHUNKS):
         w_copy(q).start()
 
@@ -111,6 +127,12 @@
         return pltpu.make_async_remote_copy(
             src_ref=acc.at[s, pl.ds(pl.multiple_of(dst * pm, pm), pm)], dst_ref=rs.at[s, src],
             send_sem=rs_send.at[s, dst], recv_sem=rs_recv.at[s, src],
+            device_id=dev, device_id_type=MESH)
+
+    def xs_copy(s, src, dst, dev):
+        return pltpu.make_async_remote_copy(
+            src_ref=xs.at[s, src], dst_ref=xs.at[s, src],
+            send_sem=xs_send.at[s, dst], recv_sem=xs_recv.at[s, src],
             device_id=dev, device_id_type=MESH)
 
     def st_copy(src, dst, dev):
@@ -164,9 +186,33 @@
             acc[s] += piece
 
     def send_sums(s):
-        for j in range(1, M):
-            dst, dev = member(j)
-            rs_copy(s, m, dst, dev).start()
+        for j in range(1, S):
+            dst, dev = core(j)
+            rs_copy(s, s_, dst, dev).start()
+
+    def cross(s):
+        h = acc[s, pl.ds(pl.multiple_of(s_ * pm, pm), pm)]
+        for j in range(1, S):
+            src, dev = core(j)
+            rs_copy(s, src, s_, dev).wait_recv()
+            h = h + rs[s, src]
+        xs[s, t] = h
+        for j in range(1, T):
+            dst, dev = across(j)
+            xs_copy(s, t, dst, dev).start()
+
+    def cross_step(d):
+        if isinstance(d, int) and d == 0:
+            cross(z)
+            return
+
+        @pl.when(z - d >= 0)
+        def _():
+            cross(z - d)
+
+        @pl.when(z + d < R)
+        def _():
+            cross(z + d)
 
     for q in range(CHUNKS):
         w_copy(q).wait()
@@ -201,6 +247,9 @@
             def _():
                 multiply(right, q)
 
+            if q == 0:
+                cross_step(d - 1)
+
         @pl.when(left >= 0)
         def _():
             send_sums(left)
@@ -222,10 +271,12 @@
             tm_copy(m, dst, dev).start()
 
     step(1)
+    for c in small:
+        c.wait()
     target_out()
 
     row = lax.broadcasted_iota(jnp.int32, (mine, total), 0)
-    position = (row // pm) * rows + m * pm + lax.rem(row, pm)
+    position = (row // pm) * rows + s_ * pm + lax.rem(row, pm)
     rank = lax.broadcasted_iota(jnp.int32, (1, total), 1)
     trainer = jnp.zeros((1, total), jnp.int32)
     start = jnp.zeros((1, total), jnp.int32)
@@ -260,26 +311,30 @@
 
     if R > 2:
         step(R - 1)
-
-    gain = gain_ref[:, own_cols]
+    cross_step(R - 1)
+
+    gain = gain_ref[...]
     lane = lax.broadcasted_iota(jnp.int32, (pm, 128), 1)
 
     def collect(s, c):
-        h = acc[s, pl.ds(pl.multiple_of(m * pm, pm), pm)]
-        for j in range(1, M):
-            src, dev = member(j)
-            rs_copy(s, src, m, dev).wait_recv()
-            h = h + rs[s, src]
+        for j in range(1, T):
+            src, dev = across(j)
+            xs_copy(s, src, t, dev).wait_recv()
+        h = xs[s, 0]
+        for q in range(1, T):
+            h = h + xs[s, q]
         here = pl.ds(pl.multiple_of(s * pm, pm), pm)
         hid[here] = h
         gh = gain * h
         a = jnp.sum(h * h, axis=1, keepdims=True)
         b = jnp.sum(gh * gh, axis=1, keepdims=True)
         e = jnp.sum(gh * tsel[here], axis=1, keepdims=True)
-        stats[z, here] = jnp.where(lane == 0, a, jnp.where(lane == 1, b, e))
+        rowsum[here] = jnp.where(lane == 0, a, jnp.where(lane == 1, b, e))
         return c
 
     lax.fori_loop(0, R, collect, 0)
+
+    stats[z] = rowsum[...].T[0:8]
 
     def send_stats(j):
         dst, dev = zpeer(j)
@@ -294,17 +349,20 @@
     each_z(got_stats)
     summed = jnp.sum(stats[...], axis=0)
     depth = R * cols
-    a, b, e = summed[:, 0:1], summed[:, 1:2], summed[:, 2:3]
+    a, b, e = summed[0:1], summed[1:2], summed[2:3]
     rstat = lax.rsqrt(a / depth + 1e-06)
     scale = 1.0 / math.sqrt(total)
     dotted = (rstat * b - e) * (scale / depth)
+    line = lax.broadcasted_iota(jnp.int32, (128, mine), 0)
+    factor = jnp.where(line == 0, rstat, rstat * rstat * rstat * dotted).T
+    rstat, pull = factor[:, 0:1], factor[:, 1:2]
     h = hid[...]
     err = h * rstat * gain - tsel[...]
-    dh = rstat * (gain * (err * scale)) - h * (rstat * rstat * rstat * dotted)
-    ag[m] = dh.astype(BF16)
-    for j in range(1, M):
-        dst, dev = member(j)
-        ag_copy(m, dst, dev).start()
+    dh = rstat * (gain * (err * scale)) - h * pull
+    ag[s_] = dh.astype(BF16)
+    for j in range(1, S):
+        dst, dev = core(j)
+        ag_copy(s_, dst, dev).start()
 
     loss = jnp.sum(err * err, axis=1, keepdims=True) / depth
     seat1 = lax.broadcasted_iota(jnp.int32, (mine, cap), 1)
@@ -329,23 +387,20 @@
         lz_copy(src, z, dev).wait_recv()
 
     each_z(got_loss)
-    lm[m] = jnp.sum(lz[...], axis=0)
-    for j in range(1, M):
-        dst, dev = member(j)
-        lm_copy(m, dst, dev).start()
-
-    for j in range(1, M):
-        src, dev = member(j)
-        ag_copy(src, m, dev).wait_recv()
-    if direct:
-        for q in range(M):
-            for s in range(R):
-                grad_out[s * rows + q * pm:s * rows + (q + 1) * pm] = ag[q, s * pm:(s + 1) * pm]
-    else:
-        grad_out[...] = ag[...]
-    for j in range(1, M):
-        src, dev = member(j)
-        lm_copy(src, m, dev).wait_recv()
+    lm[s_] = jnp.sum(lz[...], axis=0)
+    for j in range(1, S):
+        dst, dev = core(j)
+        lm_copy(s_, dst, dev).start()
+
+    for j in range(1, S):
+        src, dev = core(j)
+        ag_copy(src, s_, dev).wait_recv()
+    for q in range(S):
+        for s in range(R):
+            grad_out[s * rows + q * pm:s * rows + (q + 1) * pm] = ag[q, s * pm:(s + 1) * pm]
+    for j in range(1, S):
+        src, dev = core(j)
+        lm_copy(src, s_, dev).wait_recv()
     loss_out[...] = jnp.sum(lm[...], axis=0)
 
     def sent(s, c):
@@ -360,17 +415,22 @@
             def _():
                 f_copy(1, s, q).wait_send()
 
-        for j in range(1, M):
-            dst, dev = member(j)
-            rs_copy(s, m, dst, dev).wait_send()
+        for j in range(1, S):
+            dst, dev = core(j)
+            rs_copy(s, s_, dst, dev).wait_send()
+        for j in range(1, T):
+            dst, dev = across(j)
+            xs_copy(s, t, dst, dev).wait_send()
         return c
 
     lax.fori_loop(0, R, sent, 0)
     for j in range(1, M):
         dst, dev = member(j)
         tm_copy(m, dst, dev).wait_send()
-        ag_copy(m, dst, dev).wait_send()
-        lm_copy(m, dst, dev).wait_send()
+    for j in range(1, S):
+        dst, dev = core(j)
+        ag_copy(s_, dst, dev).wait_send()
+        lm_copy(s_, dst, dev).wait_send()
 
     def sent_z(j):
         dst, dev = zpeer(j)
@@ -379,6 +439,11 @@
         lz_copy(z, dst, dev).wait_send()
 
     each_z(sent_z)
+
+
+def outer(f_ref, g_ref, out_ref):
+    out_ref[...] = lax.dot_general(
+        f_ref[...], g_ref[...], (((0,), (0,)), ((), ())), preferred_element_type=F32)
 
 
 def on_device(features, fc_weight, counts, order, norm_gain, target):
@@ -392,53 +457,65 @@
     share = target.shape[0]
     cap = share * M
     part = depth // CHUNKS
-    pm = rows // M
+    pm = rows // S
     mine = R * pm
-    direct = pm % 16 == 0
     any_ = pl.BlockSpec(memory_space=pl.ANY)
+    hbm = pl.BlockSpec(memory_space=pltpu.HBM)
     vmem = pl.BlockSpec(memory_space=pltpu.VMEM)
-    smem = pl.BlockSpec(memory_space=pltpu.SMEM)
     dma = pltpu.SemaphoreType.DMA
-    grad_shape = (total, cols) if direct else (M, mine, cols)
     all_features, grad, loss = pl.pallas_call(
-        functools.partial(kernel, R, T, S, direct),
+        functools.partial(kernel, R, T, S),
         out_shape=(
             jax.ShapeDtypeStruct((total, depth), BF16),
-            jax.ShapeDtypeStruct(grad_shape, BF16),
+            jax.ShapeDtypeStruct((total, cols), BF16),
             jax.ShapeDtypeStruct((8, cap), F32),
         ),
-        in_specs=[smem, vmem, vmem, any_, any_, any_],
+        in_specs=[hbm] * 6,
         out_specs=(any_, vmem, vmem),
         scratch_shapes=[
+            pltpu.SMEM((R,), jnp.int32),
+            pltpu.VMEM((1, total), jnp.int32),
+            pltpu.VMEM((1, cols), F32),
             pltpu.VMEM((R, CHUNKS, rows, part), BF16),
             pltpu.VMEM((CHUNKS, part, cols), BF16),
             pltpu.VMEM((R, rows, cols), F32),
-            pltpu.VMEM((R, M, pm, cols), F32),
+            pltpu.VMEM((R, S, pm, cols), F32),
+            pltpu.VMEM((R, T, pm, cols), F32),
             pltpu.VMEM((M, R, share, cols), BF16),
             pltpu.VMEM((mine, cols), F32),
             pltpu.VMEM((mine, cols), F32),
-            pltpu.VMEM((R, mine, 128), F32),
-            pltpu.VMEM((M, mine, cols), BF16),
+            pltpu.VMEM((mine, 128), F32),
+            pltpu.VMEM((R, 8, mine), F32),
+            pltpu.VMEM((S, mine, cols), BF16),
             pltpu.VMEM((R, 8, cap), F32),
             pltpu.VMEM((R, 8, cap), F32),
-            pltpu.VMEM((M, 8, cap), F32),
+            pltpu.VMEM((S, 8, cap), F32),
             dma((CHUNKS,)), dma((CHUNKS,)), dma((R, CHUNKS)),
             dma((2, R, CHUNKS)), dma((R, CHUNKS)),
-            dma((R, M)), dma((R, M)),
+            dma((R, S)), dma((R, S)), dma((R, T)), dma((R, T)),
             dma((R,)), dma((R,)), dma((M,)), dma((M,)),
-            dma((R,)), dma((R,)), dma((M,)), dma((M,)),
-            dma((R,)), dma((R,)), dma((M,)), dma((M,)), dma((1,)),
+            dma((R,)), dma((R,)), dma((S,)), dma((S,)),
+            dma((R,)), dma((R,)), dma((S,)), dma((S,)), dma((4,)),
         ],
         compiler_params=pltpu.CompilerParams(
             collective_id=0, has_side_effects=True, vmem_limit_bytes=48 * 1024 * 1024),
         name="gather_join_norm",
     )(counts, order[None, :], norm_gain[None, :], features, fc_weight, target)
-    if not direct:
-        grad = grad.reshape(M, R, pm, cols).transpose(1, 0, 2, 3).reshape(total, cols)
     member = lax.axis_index("tensor") * S + lax.axis_index("sub")
     loss_slots = lax.dynamic_slice_in_dim(loss[0], member * share, share, 0)
-    fc_grad = lax.dot_general(
-        all_features, grad, (((0,), (0,)), ((), ())), preferred_element_type=F32)
+    tile = depth // 12
+    fc_grad = pl.pallas_call(
+        outer,
+        grid=(depth // tile,),
+        out_shape=jax.ShapeDtypeStruct((depth, cols), F32),
+        in_specs=[
+            pl.BlockSpec((total, tile), lambda i: (0, i)),
+            pl.BlockSpec((total, cols), lambda i: (0, 0)),
+        ],
+        out_specs=pl.BlockSpec((tile, cols), lambda i: (i, 0)),
+        compiler_params=pltpu.CompilerParams(vmem_limit_bytes=32 * 1024 * 1024),
+        name="weight_gradient",
+    )(all_features, grad)
     return (fc_grad, loss_slots)
 
 

time: 97 us -> 94.2 us (0.971)
  matrix products: 10.8 us -> 0 us
  Pallas kernels: 80.5 us -> 88.5 us
    dot_general x1 -> x0, matrix products: 10.8 us -> none  [on_device(): lax.dot_general(all_features, grad, (((0,), (0,)), ((), ())), preferred_e...]
    pallas_call x1 -> x2, Pallas kernels: 80.5 us -> 88.5 us  [the longest x1 77 us: on_device(): pl.pallas_call(functools.partial(kernel, R, T, S), out_shape=(jax.ShapeDt...]
where the time goes in v2:
time: 94.2 us; the launch traced here: 93.9 us
  Pallas kernels  88.5 us (94%)
  local copies, waits for them, and re-layouts  4.72 us (5%)
    pallas_call x1, Pallas kernels, on_device(): pl.pallas_call(functools.partial(kernel, R, T, S), out_shape=(jax.ShapeDt...  77 us
    pallas_call x1, Pallas kernels, on_device(): pl.pallas_call(outer, grid=(depth // tile,), out_shape=jax.ShapeDtypeStru...  11.5 us
    unnamed x10, local copies, waits for them, and re-layouts  4.13 us

profile of v2, /device:TPU:0, one launch (start us, length us, event | category | flops | bytes accessed | tf_op | source)
XLA Modules:
  0.0 93.9 jit_solution(550813649585455685)
XLA Ops:
  0.6 0.0 copy-start
  0.6 1.1 %copy-done = bf16[64,6144]{1,0:T(8,128)(2,1)S(1)} copy-done((bf16[64,6144]{1,0:T(8,128)(2,1)S(1)}, bf16[64,6144]{1,0:T(8,128)(2,1)}, u32[]{:S(2)}) %copy-start) | copy-done | bytes 786456
  1.8 0.0 copy-start.1
  1.8 0.9 %copy-done.1 = bf16[32,4096]{1,0:T(8,128)(2,1)S(1)} copy-done((bf16[32,4096]{1,0:T(8,128)(2,1)S(1)}, bf16[32,4096]{1,0:T(8,128)(2,1)}, u32[]{:S(2)}) %copy-start.1) | copy-done | bytes 262168
  2.7 0.0 copy-start.2
  2.7 0.7 copy-done.2
  3.4 0.0 copy-start.3
  3.4 0.7 copy-done.3
  4.1 0.0 copy-start.4
  4.1 0.7 copy-done.4
  4.8 77.0 %gather_join_norm.1 = (bf16[256,6144]{1,0:T(8,128)(2,1)S(1)}, bf16[256,1024]{1,0:T(8,128)(2,1)S(1)}, f32[8,128]{1,0:T(8,128)S(1)}) custom-call(s32[4]{0:T(128)S(1)} %copy-done.4, s32[1,256]{1,0:T(1,128)S(1)} %bitcast.5, f32[1,4096]{1,0:T(1,128)S(1)} %bitcast.4, bf16[64,6144]{1,0:T(8,128)(2,1)S(1)} %copy-done, bf16[6144,1024]{1,0:T(8,128)(2,1)} %w_in.1, ...), custom_call_target="tpu_custom_call" | custom-call | tf_op jit(solution)/shard_map/gather_join_norm/pallas_call | solution.py:466
  81.8 0.6 dynamic-slice_bitcast_fusion
  82.4 11.5 %weight_gradient.1 = f32[6144,1024]{1,0:T(8,128)} custom-call(bf16[256,6144]{1,0:T(8,128)(2,1)S(1)} %get-tuple-element.5.f_ref, bf16[256,1024]{1,0:T(8,128)(2,1)S(1)} %get-tuple-element.6.g_ref), custom_call_target="tpu_custom_call" | custom-call | tf_op jit(solution)/shard_map/weight_gradient/pallas_call | solution.py:507
  (1 shorter events, 0.0 us)
Async XLA Ops:
  0.6 1.1 %copy-start = (bf16[64,6144]{1,0:T(8,128)(2,1)S(1)}, bf16[64,6144]{1,0:T(8,128)(2,1)}, u32[]{:S(2)}) copy-start(bf16[64,6144]{1,0:T(8,128)(2,1)} %feat_in.1) | copy-start | bytes 2359300
  1.8 0.9 %copy-start.1 = (bf16[32,4096]{1,0:T(8,128)(2,1)S(1)}, bf16[32,4096]{1,0:T(8,128)(2,1)}, u32[]{:S(2)}) copy-start(bf16[32,4096]{1,0:T(8,128)(2,1)} %target_in.1) | copy-start | bytes 786436
  2.7 0.7 copy-start.2
  3.4 0.7 copy-start.3
  4.1 0.7 copy-start.4

commit v3 on v2

--- a/solution.py
+++ b/solution.py
@@ -358,28 +358,28 @@
     rstat, pull = factor[:, 0:1], factor[:, 1:2]
     h = hid[...]
     err = h * rstat * gain - tsel[...]
+    loss = jnp.sum(err * err, axis=1, keepdims=True) / depth
+    seat1 = lax.broadcasted_iota(jnp.int32, (mine, cap), 1)
+
+    def scatter(r, c):
+        one = jnp.sum(
+            jnp.where(slot - r * cap == seat1, loss, F32(0)), axis=0, keepdims=True)
+        lp[r] = jnp.broadcast_to(one, (8, cap))
+        return c
+
+    lax.fori_loop(0, R, scatter, 0)
+
+    def send_loss(j):
+        dst, dev = zpeer(j)
+        lz_copy(z, dst, dev).start()
+
+    each_z(send_loss)
     dh = rstat * (gain * (err * scale)) - h * pull
     ag[s_] = dh.astype(BF16)
     for j in range(1, S):
         dst, dev = core(j)
         ag_copy(s_, dst, dev).start()
 
-    loss = jnp.sum(err * err, axis=1, keepdims=True) / depth
-    seat1 = lax.broadcasted_iota(jnp.int32, (mine, cap), 1)
-
-    def scatter(r, c):
-        one = jnp.sum(
-            jnp.where(slot - r * cap == seat1, loss, F32(0)), axis=0, keepdims=True)
-        lp[r] = jnp.broadcast_to(one, (8, cap))
-        return c
-
-    lax.fori_loop(0, R, scatter, 0)
-
-    def send_loss(j):
-        dst, dev = zpeer(j)
-        lz_copy(z, dst, dev).start()
-
-    each_z(send_loss)
     lz[z] = lp[z]
 
     def got_loss(j):
@@ -498,12 +498,12 @@
             dma((R,)), dma((R,)), dma((S,)), dma((S,)), dma((4,)),
         ],
         compiler_params=pltpu.CompilerParams(
-            collective_id=0, has_side_effects=True, vmem_limit_bytes=48 * 1024 * 1024),
+            collective_id=0, has_side_effects=True, vmem_limit_bytes=60 * 1024 * 1024),
         name="gather_join_norm",
     )(counts, order[None, :], norm_gain[None, :], features, fc_weight, target)
     member = lax.axis_index("tensor") * S + lax.axis_index("sub")
     loss_slots = lax.dynamic_slice_in_dim(loss[0], member * share, share, 0)
-    tile = depth // 12
+    tile = depth // 4
     fc_grad = pl.pallas_call(
         outer,
         grid=(depth // tile,),

time: 94.2 us -> 92.4 us (0.981)
  Pallas kernels: 88.5 us -> 87.3 us
    pallas_call x1, Pallas kernels: 11.5 us -> 9.69 us  [on_device(): pl.pallas_call(outer, grid=(depth // tile,), out_shape=jax.ShapeDtypeStru...]
    unnamed x10 -> x4, local copies, waits for them, and re-layouts: 4.13 us -> 2.93 us
where the time goes in v3:
time: 92.4 us; the launch traced here: 92.1 us
  Pallas kernels  87.3 us (94%)
  local copies, waits for them, and re-layouts  4.19 us (5%)
    pallas_call x1, Pallas kernels, on_device(): pl.pallas_call(functools.partial(kernel, R, T, S), out_shape=(jax.ShapeDt...  77.6 us
    pallas_call x1, Pallas kernels, on_device(): pl.pallas_call(outer, grid=(depth // tile,), out_shape=jax.ShapeDtypeStru...  9.69 us
    unnamed x4, local copies, waits for them, and re-layouts  2.93 us

profile of v3, /device:TPU:0, one launch (start us, length us, event | category | flops | bytes accessed | tf_op | source)
XLA Modules:
  0.0 92.1 jit_solution(18047013656394288929)
XLA Ops:
  0.6 77.6 %gather_join_norm.1 = (bf16[256,6144]{1,0:T(8,128)(2,1)}, bf16[256,1024]{1,0:T(8,128)(2,1)}, f32[8,128]{1,0:T(8,128)}) custom-call(s32[4]{0:T(128)} %counts_in.1, s32[1,256]{1,0:T(1,128)} %bitcast.5, f32[1,4096]{1,0:T(1,128)} %bitcast.4, bf16[64,6144]{1,0:T(8,128)(2,1)} %feat_in.1, bf16[6144,1024]{1,0:T(8,128)(2,1)} %w_in.1, bf16[32,4096]{1,0:T(8,128)(2,1)} %target_in.1), custom_call_target="tpu_custom_call" | custom-call | tf_op jit(solution)/shard_map/gather_join_norm/pallas_call | solution.py:466
  78.3 0.7 slice.3
  78.9 0.6 dynamic-slice_bitcast_fusion
  79.5 0.0 copy-start
  79.5 1.9 %copy-done = bf16[256,6144]{1,0:T(8,128)(2,1)S(1)} copy-done((bf16[256,6144]{1,0:T(8,128)(2,1)S(1)}, bf16[256,6144]{1,0:T(8,128)(2,1)}, u32[]{:S(2)}) %copy-start) | copy-done | bytes 3145752
  81.4 0.0 copy-start.1
  81.4 1.0 %copy-done.1 = bf16[256,1024]{1,0:T(8,128)(2,1)S(1)} copy-done((bf16[256,1024]{1,0:T(8,128)(2,1)S(1)}, bf16[256,1024]{1,0:T(8,128)(2,1)}, u32[]{:S(2)}) %copy-start.1) | copy-done | bytes 524312
  82.5 9.7 %weight_gradient.1 = f32[6144,1024]{1,0:T(8,128)} custom-call(bf16[256,6144]{1,0:T(8,128)(2,1)S(1)} %copy-done, bf16[256,1024]{1,0:T(8,128)(2,1)S(1)} %copy-done.1), custom_call_target="tpu_custom_call" | custom-call | tf_op jit(solution)/shard_map/weight_gradient/pallas_call | solution.py:507
Async XLA Ops:
  79.5 1.9 %copy-start = (bf16[256,6144]{1,0:T(8,128)(2,1)S(1)}, bf16[256,6144]{1,0:T(8,128)(2,1)}, u32[]{:S(2)}) copy-start(bf16[256,6144]{1,0:T(8,128)(2,1)} %get-tuple-element.5.f_ref) | copy-start | bytes 9437188
  81.4 1.0 %copy-start.1 = (bf16[256,1024]{1,0:T(8,128)(2,1)S(1)}, bf16[256,1024]{1,0:T(8,128)(2,1)}, u32[]{:S(2)}) copy-start(bf16[256,1024]{1,0:T(8,128)(2,1)} %get-tuple-element.6.g_ref) | copy-start | bytes 1572868
